TPU v7x, 32 devices: a whole 2x2x4 slice. The times are simulated.
32 devices in a mesh: grp: 2 (over y), seq: 4 (over z), blk: 2 (over x), rep: 2 (over core).
Axes of the slice: x: 2, y: 2, z: 4, core: 2. Of those that a mesh axis runs over, the one named last changes fastest.
Arguments:
- q_proj: bfloat16 [8, 2048, 512], P(('grp', 'blk', 'rep'), 'seq'), parts along dimension 0, may hold values from -6 to 6
- k_proj: bfloat16 [8, 2048, 128], P(('grp', 'blk', 'rep'), 'seq'), parts along dimension 0, may hold values from -6 to 6
- v_proj: bfloat16 [8, 2048, 128], P(('grp', 'blk', 'rep'), 'seq'), parts along dimension 0, may hold values from -6 to 6
- q_gain: float32 [128], replicated, may hold values from 0.5 to 1.5
- k_gain: float32 [128], replicated, may hold values from 0.5 to 1.5
- out_weight: bfloat16 [512, 2560], P('seq'), may hold values from -0.25 to 0.25
- lengths: int32 [8, 1], P(('grp', 'blk', 'rep')), parts along dimension 0, may hold values from 512 to 2048, as said below
- query_emb: bfloat16 [512, 2560], P(('grp', 'blk')), parts along dimension 0, may hold values from -6 to 6
- teacher: float32 [512, 4], P(('grp', 'blk')), parts along dimension 0, may hold values from -16 to 16
Outputs:
- q_grad: bfloat16 [8, 2048, 512], P(('grp', 'blk', 'rep'), 'seq'), parts along dimension 0
- k_grad: bfloat16 [8, 2048, 128], P(('grp', 'blk', 'rep'), 'seq'), parts along dimension 0
- v_grad: bfloat16 [8, 2048, 128], P(('grp', 'blk', 'rep'), 'seq'), parts along dimension 0
- weight_grad: bfloat16 [1024, 2560], P(('grp', 'seq')), parts along dimension 0
- row_loss: float32 [512], P(('grp', 'blk')), parts along dimension 0
- col_loss: float32 [8], P('grp'), parts along dimension 0
There are 2 independent parts, one for each index of `grp`. A program takes and returns all parts, laid end to end along the dimension named above; an argument that names none is the same for every part. Nothing has to cross between parts.
Inputs may be any that keep to these rules, and one draw needn't show every extreme that they name: `lengths`: live tokens of each passage, counted from its first position; the rest is padding.
All inputs are finite; a program needn't handle non-finite values.
Results may differ from a plain program's by a relative error of at most 0.017.
Values may be sent and summed in bfloat16 or wider, within the bound.
A program may use at most 64 MiB of HBM per device.

v0:
```python
import math
import jax
import jax.numpy as jnp
from jax import lax
from jax.sharding import PartitionSpec as P

HD = 128
PASS_LEN = 2048
logit_divisor = 0.05


def rms_scale(wide):
    return lax.rsqrt(jnp.mean(wide * wide, axis=-1, keepdims=True) + 1e-06)


def normed(source, gain_weights):
    wide = source.astype(jnp.float32)
    return (wide * rms_scale(wide) * gain_weights).astype(jnp.bfloat16)


def norm_back(source, gain_weights, grad_out):
    wide = source.astype(jnp.float32)
    inv_rms = rms_scale(wide)
    scaled_grad = gain_weights * grad_out
    return (
        inv_rms * scaled_grad
        - wide * inv_rms**3 * jnp.mean(scaled_grad * wide, axis=-1, keepdims=True)
    ).astype(jnp.bfloat16)


def shards(q_proj, k_proj, v_proj, q_gain, k_gain, out_weight, lengths, query_emb, teacher):
    number_of_sequences = lax.axis_size("seq")
    blk_count = lax.axis_size("blk")
    tok_dev = q_proj.shape[1]
    heads_all = q_proj.shape[2] // HD
    kv_heads = k_proj.shape[2] // HD
    group_size = heads_all // kv_heads
    local_heads = out_weight.shape[0] // HD
    group_tok = tok_dev * number_of_sequences
    passes = group_tok // PASS_LEN
    pass_lens = lengths[0]
    inv_root = 1.0 / math.sqrt(HD)
    block_rows = min(512, PASS_LEN)
    block_count = PASS_LEN // block_rows

    def widen(rows):
        spread = jnp.broadcast_to(
            rows.reshape(tok_dev, kv_heads, 1, HD), (tok_dev, kv_heads, group_size, HD)
        )
        return spread.reshape(tok_dev, heads_all * HD)

    q_heads, k_heads, v_heads = (
        lax.all_to_all(q_proj[0], "seq", split_axis=1, concat_axis=0, tiled=True),
        lax.all_to_all(widen(k_proj[0]), "seq", split_axis=1, concat_axis=0, tiled=True),
        lax.all_to_all(widen(v_proj[0]), "seq", split_axis=1, concat_axis=0, tiled=True),
    )
    head_shape = (passes, PASS_LEN, local_heads, HD)
    q_raw = q_heads.reshape(head_shape)
    k_raw = k_heads.reshape(head_shape)
    v_all = v_heads.reshape(head_shape)
    q_unit = normed(q_raw, q_gain)
    k_unit = normed(k_raw, k_gain)
    positions = lax.iota(jnp.int32, PASS_LEN)
    passage = 0
    q_block = q_unit[passage]
    k_block = k_unit[passage]
    stored = []
    for attend_index in range(block_count):
        attend_ending = (attend_index + 1) * block_rows
        rows_here = q_block[attend_index * block_rows : attend_ending]
        logits = (
            jnp.einsum(
                "thd,uhd->htu",
                rows_here,
                k_block[:attend_ending],
                preferred_element_type=jnp.float32,
            )
            * inv_root
        )
        causal = (attend_index * block_rows + lax.iota(jnp.int32, block_rows))[:, None] >= lax.iota(
            jnp.int32, attend_ending
        )[None, :]
        powers = jnp.where(causal[None], jnp.exp(logits), 0.0)
        stored.append(
            lax.optimization_barrier(
                (powers / jnp.sum(powers, axis=2, keepdims=True)).astype(jnp.bfloat16)
            )
        )
    blocks = stored
    saved_blocks = [blocks]
    live_len = pass_lens[passage]
    live_mask = (positions < live_len).astype(jnp.bfloat16)
    col_weight = jnp.zeros((local_heads, PASS_LEN), jnp.float32)
    for index in range(block_count):
        ending = (index + 1) * block_rows
        column_part = jnp.einsum(
            "t,htu->hu",
            live_mask[index * block_rows : ending],
            blocks[index],
            preferred_element_type=jnp.float32,
        )
        col_weight = col_weight.at[:, :ending].add(column_part)
    col_weight = col_weight / live_len.astype(jnp.float32)
    pooled_list = [jnp.sum(col_weight.T[:, :, None] * v_all[passage].astype(jnp.float32), axis=0)]
    weight_list = [col_weight.astype(jnp.bfloat16)]
    pooled = jnp.stack(pooled_list)
    col_weights = jnp.stack(weight_list)
    pooled_flat = pooled.reshape(passes, local_heads * HD).astype(jnp.bfloat16)
    partial_value = jnp.dot(pooled_flat, out_weight, preferred_element_type=jnp.float32)
    summed = lax.psum(partial_value, "seq")
    inv_norm = lax.rsqrt(jnp.sum(summed * summed, axis=1, keepdims=True) + 1e-06)
    passage_unit = summed * inv_norm
    passage_all = lax.all_gather(
        passage_unit.astype(jnp.bfloat16), ("blk", "rep"), axis=0, tiled=True
    )
    query_wide = query_emb.astype(jnp.float32)
    request_unit_length = (
        query_wide * lax.rsqrt(jnp.sum(query_wide * query_wide, axis=1, keepdims=True) + 1e-06)
    ).astype(jnp.bfloat16)
    learner_similarities = (
        lax.dot_general(
            request_unit_length,
            passage_all,
            (((1,), (1,)), ((), ())),
            preferred_element_type=jnp.float32,
        )
        / logit_divisor
    )
    exp_student = jnp.exp(learner_similarities)
    exp_teacher = jnp.exp(teacher)
    row_student = jnp.sum(exp_student, axis=1, keepdims=True)
    row_teacher = jnp.sum(exp_teacher, axis=1, keepdims=True)
    gap = exp_teacher * (teacher - learner_similarities)
    col_student, col_teacher, col_gap = lax.psum(
        (jnp.sum(exp_student, axis=0), jnp.sum(exp_teacher, axis=0), jnp.sum(gap, axis=0)), "blk"
    )
    row_loss = (
        jnp.sum(gap, axis=1) / row_teacher[:, 0]
        - jnp.log(row_teacher[:, 0])
        + jnp.log(row_student[:, 0])
    )
    col_loss = col_gap / col_teacher - jnp.log(col_teacher) + jnp.log(col_student)
    query_total = query_emb.shape[0] * blk_count
    passage_total = teacher.shape[1]
    similarity_derivative = (
        (exp_student / row_student - exp_teacher / row_teacher) / query_total
        + (exp_student / col_student - exp_teacher / col_teacher) / passage_total
    ).astype(jnp.bfloat16)
    grad_block = lax.psum_scatter(
        (
            lax.dot_general(
                similarity_derivative,
                request_unit_length,
                (((0,), (0,)), ((), ())),
                preferred_element_type=jnp.float32,
            )
            / logit_divisor
        ).astype(jnp.bfloat16),
        "blk",
        scatter_dimension=0,
        tiled=True,
    ).astype(jnp.float32)
    representation_derivative = lax.dynamic_slice_in_dim(
        grad_block, lax.axis_index("rep") * passes, passes, 0
    )
    grad_sum = (
        (
            representation_derivative
            - passage_unit
            * jnp.sum(passage_unit * representation_derivative, axis=1, keepdims=True)
        )
        * inv_norm
    ).astype(jnp.bfloat16)
    pooled_every, grads_every = (
        lax.all_gather(pooled_flat, ("blk", "rep"), axis=0, tiled=True),
        lax.all_gather(grad_sum, ("blk", "rep"), axis=0, tiled=True),
    )
    weight_grad = lax.dot_general(
        pooled_every, grads_every, (((0,), (0,)), ((), ())), preferred_element_type=jnp.float32
    ).astype(jnp.bfloat16)
    grad_pool = lax.dot_general(
        grad_sum, out_weight, (((1,), (1,)), ((), ())), preferred_element_type=jnp.float32
    )
    pool_heads = grad_pool.reshape(passes, local_heads, HD)
    passage = 0
    blocks = saved_blocks[passage]
    q_block = q_unit[passage]
    k_block = k_unit[passage]
    live_len = pass_lens[passage]
    live_mask = (positions < live_len).astype(jnp.float32) / live_len.astype(jnp.float32)
    value_dot = jnp.sum(v_all[passage].astype(jnp.float32) * pool_heads[passage][None], axis=2).T
    grad_k_copy = jnp.zeros((PASS_LEN, local_heads, HD), jnp.float32)
    query_parts = []
    for index in range(block_count):
        ending = (index + 1) * block_rows
        stored_block = blocks[index]
        value_here = value_dot[:, None, :ending]
        mean_dot = jnp.sum(stored_block.astype(jnp.float32) * value_here, axis=2)
        local_live_mask = live_mask[index * block_rows : ending]
        grad_logits = (
            stored_block.astype(jnp.float32)
            * local_live_mask[None, :, None]
            * (value_here - mean_dot[:, :, None])
            * inv_root
        ).astype(jnp.bfloat16)
        query_parts.append(
            jnp.einsum(
                "htu,uhd->thd", grad_logits, k_block[:ending], preferred_element_type=jnp.float32
            )
        )
        key_part = jnp.einsum(
            "htu,thd->uhd",
            grad_logits,
            q_block[index * block_rows : ending],
            preferred_element_type=jnp.float32,
        )
        grad_k_copy = grad_k_copy.at[:ending].add(key_part)
    grad_q_unit = jnp.concatenate(query_parts, axis=0)
    q_list = [norm_back(q_raw[passage], q_gain, grad_q_unit)]
    k_list = [norm_back(k_raw[passage], k_gain, grad_k_copy)]
    q_terms = jnp.stack(q_list)
    k_terms = jnp.stack(k_list)
    flat_shape = (group_tok, local_heads * HD)

    def narrow(terms):
        wide = terms.astype(jnp.float32).reshape(tok_dev, kv_heads, group_size, HD)
        return jnp.sum(wide, axis=2).astype(jnp.bfloat16).reshape(tok_dev, kv_heads * HD)

    q_back, k_back, v_back = (
        lax.all_to_all(q_terms.reshape(flat_shape), "seq", split_axis=0, concat_axis=1, tiled=True),
        lax.all_to_all(k_terms.reshape(flat_shape), "seq", split_axis=0, concat_axis=1, tiled=True),
        lax.all_to_all(
            (col_weights.astype(jnp.float32).transpose(0, 2, 1)[..., None] * pool_heads[:, None])
            .astype(jnp.bfloat16)
            .reshape(flat_shape),
            "seq",
            split_axis=0,
            concat_axis=1,
            tiled=True,
        ),
    )
    k_out = narrow(k_back)
    v_out = narrow(v_back)
    return (q_back[None], k_out[None], v_out[None], weight_grad, row_loss, col_loss)


def solution(mesh):
    placed = (
        P(("grp", "blk", "rep"), "seq", None),
        P(("grp", "blk", "rep"), "seq", None),
        P(("grp", "blk", "rep"), "seq", None),
        P(),
        P(),
        P("seq", None),
        P(("grp", "blk", "rep"), None),
        P(("grp", "blk"), None),
        P(("grp", "blk"), None),
    )
    return jax.shard_map(
        shards,
        mesh=mesh,
        in_specs=placed,
        out_specs=(
            P(("grp", "blk", "rep"), "seq", None),
            P(("grp", "blk", "rep"), "seq", None),
            P(("grp", "blk", "rep"), "seq", None),
            P(("grp", "seq"), None),
            P(("grp", "blk")),
            P("grp"),
        ),
        check_vma=False,
    )
```

profile of v0, /device:TPU:0, one launch (start us, length us, event | category | flops | bytes accessed | tf_op | source)
XLA Modules:
  0.0 180.6 jit_solution(1321558911935933446)
XLA Ops:
  2.7 6.3 %all-to-all-start.1 = ((bf16[512,4,128]{0,2,1:T(8,128)(2,1)}), bf16[512,4,128]{0,2,1:T(8,128)(2,1)S(1)}, u32[]{:S(2)}, u32[]{:S(2)}) async-start(bf16[512,4,128]{0,2,1:T(8,128)(2,1)} %broadcast_in_dim.25), calls=%async_computation.1 | async-start | bytes 1048576 | tf_op jit(solution)/shard_map/all_to_all | solution.py:54
  10.7 12.7 %all-to-all-done.1 = bf16[512,4,128]{0,2,1:T(8,128)(2,1)S(1)} async-done(((bf16[512,4,128]{0,2,1:T(8,128)(2,1)}), bf16[512,4,128]{0,2,1:T(8,128)(2,1)S(1)}, u32[]{:S(2)}, u32[]{:S(2)}) %all-to-all-start.1) | async-done | bytes 524320 | tf_op jit(solution)/shard_map/all_to_all | solution.py:54
  23.5 3.5 %all-to-all-start = ((bf16[512,4,128]{0,2,1:T(8,128)(2,1)}), bf16[512,4,128]{0,2,1:T(8,128)(2,1)S(1)}, u32[]{:S(2)}, u32[]{:S(2)}) async-start(bf16[512,4,128]{0,2,1:T(8,128)(2,1)} %bitcast), calls=%async_computation | async-start | bytes 1048576 | tf_op jit(solution)/shard_map/all_to_all | solution.py:53
  31.1 9.8 %all-to-all-done = bf16[512,4,128]{0,2,1:T(8,128)(2,1)S(1)} async-done(((bf16[512,4,128]{0,2,1:T(8,128)(2,1)}), bf16[512,4,128]{0,2,1:T(8,128)(2,1)S(1)}, u32[]{:S(2)}, u32[]{:S(2)}) %all-to-all-start) | async-done | bytes 524320 | tf_op jit(solution)/shard_map/all_to_all | solution.py:53
  41.8 4.3 %all-to-all-start.2 = ((bf16[512,4,128]{2,0,1:T(8,128)(2,1)}), bf16[512,4,128]{2,0,1:T(8,128)(2,1)}, u32[]{:S(2)}, u32[]{:S(2)}) async-start(bf16[512,4,128]{2,0,1:T(8,128)(2,1)} %broadcast_in_dim.29), calls=%async_computation.2 | async-start | bytes 1048576 | tf_op jit(solution)/shard_map/all_to_all | solution.py:55
  47.9 1.4 fusion.96
  57.8 2.3 %all-to-all-done.2 = bf16[512,4,128]{2,0,1:T(8,128)(2,1)} async-done(((bf16[512,4,128]{2,0,1:T(8,128)(2,1)}), bf16[512,4,128]{2,0,1:T(8,128)(2,1)}, u32[]{:S(2)}, u32[]{:S(2)}) %all-to-all-start.2) | async-done | bytes 524320 | tf_op jit(solution)/shard_map/all_to_all | solution.py:55
  63.3 16.8 %psum.28 = f32[1,2560]{1,0:T(1,128)S(1)} all-reduce(f32[1,2560]{1,0:T(1,128)S(1)} %fusion.77), channel_id=1, replica_groups=mesh['grp'=2,'seq'=4,'blk'=2,'rep'=2] {'seq'}, use_global_device_ids=true, to_apply=%region_11.12 | all-reduce | flops 2560 | bytes 20480 | tf_op jit(solution)/shard_map/psum | solution.py:110
  81.4 5.2 %all-gather.1 = bf16[4,1,2560]{2,1,0:T(2,128)(2,1)S(1)} all-gather(bf16[1,1,2560]{2,1,0:T(2,128)(2,1)S(1)} %convert_bitcast_fusion.1), channel_id=1, replica_groups=mesh['grp'=2,'seq'=4,'blk'=2,'rep'=2] {'blk','rep'}, dimensions={0}, use_global_device_ids=true | all-gather | bytes 25600 | tf_op jit(solution)/shard_map/all_gather | solution.py:113
  86.6 2.0 %fusion.80 = (f32[4]{0:T(128)S(1)}, f32[128]{0:T(128)}, f32[4]{0:T(128)S(1)}, f32[128]{0:T(128)S(1)}, f32[4]{0:T(128)S(1)}, /*index=5*/f32[128]{0:T(128)S(1)}, f32[128,4]{0,1:T(4,128)S(1)}) fusion(f32[128,4]{0,1:T(4,128)S(1)} %copy-done.55, bf16[4,1,2560]{2,1,0:T(2,128)(2,1)S(1)} %all-gather.1, bf16[128,2560]{1,0:T(8,128)(2,1)} %param.36, ...), kind=kOutput, calls=%fused_computation.165 | convolution fusion | flops 3608692 | bytes 682032 | tf_op jit(solution)/shard_map/dot_general | solution.py:121
  88.6 5.4 %all-reduce.3 = (f32[4]{0:T(128)S(1)}, f32[4]{0:T(128)S(1)}, f32[4]{0:T(128)}) all-reduce(f32[4]{0:T(128)S(1)} %get-tuple-element.140, f32[4]{0:T(128)S(1)} %get-tuple-element.138, f32[4]{0:T(128)S(1)} %get-tuple-element.136), channel_id=1, replica_groups=mesh['grp'=2,'seq'=4,'blk'=2,'rep'=2] {'blk'}, use_global_device_ids=true, to_apply=%region_18.19 | all-reduce | flops 12 | bytes 96 | tf_op jit(solution)/shard_map/psum | solution.py:134
  94.1 1.4 fusion.4
  95.5 8.3 %all-reduce.2 = bf16[4,2560]{1,0:T(4,128)(2,1)S(1)} all-reduce(bf16[4,2560]{1,0:T(4,128)(2,1)S(1)} %fusion.4), channel_id=3, replica_groups=mesh['grp'=2,'seq'=4,'blk'=2,'rep'=2] {'blk'}, use_global_device_ids=true, to_apply=%region_19.20.clone | all-reduce | flops 10240 | bytes 40960
  105.9 1.6 fusion.44
  108.6 2.1 %convolution_bitcast_fusion.3 = f32[512,1,128]{0,2,1:T(8,128)} fusion(bf16[1,2048,1,128]{3,1,2,0:T(8,128)(2,1)} %copy-done.19, bf16[1,512,512]{1,2,0:T(8,128)(2,1)S(1)} %fusion.55, f32[512]{0:T(512)S(1)} %fusion.39, f32[512]{0:T(512)S(1)} %bitcast.270, f32[512]{0:T(512)S(1)} %get-tuple-element.148), kind=kOutput, calls=%fused_computation.61 | convolution fusion | flops 68681728 | bytes 923648 | tf_op jit(solution)/shard_map/htu,thd->uhd/dot_general | solution.py:211
  112.0 1.3 fusion.87
  118.4 2.5 %copy.54 = f32[2048,128]{1,0:T(8,128)} copy(f32[2048,128]{0,1:T(8,128)} %pad_maximum_fusion) | data formatting | bytes 2097152 | tf_op jit(solution)/shard_map/concatenate | solution.py:218
  120.9 1.3 copy.55
  122.3 1.6 fusion.42
  123.9 2.9 %fusion.49 = bf16[4,512,128]{2,1,0:T(8,128)(2,1)} fusion(f32[4,512,128]{2,1,0:T(8,128)} %bitcast.241, bf16[512,4,128]{2,0,1:T(8,128)(2,1)} %copy-done.15, f32[4,512]{1,0:T(4,128)S(1)} %div.160, f32[4,512]{1,0:T(4,128)} %get-tuple-element.147, f32[128]{0:T(128)} %param.32, f32[4,512]{1,0:T(4,128)} %get-tuple-element.145), kind=kLoop, calls=%fused_computation.86 | loop fusion | flops 1835008 | bytes 2122240 | tf_op jit(solution)/shard_map/convert_element_type | solution.py:28
  126.8 2.1 %copy.48 = bf16[4,512,128]{1,2,0:T(8,128)(2,1)} copy(bf16[4,512,128]{2,1,0:T(8,128)(2,1)} %fusion.49) | data formatting | bytes 1048576 | tf_op jit(solution)/shard_map/convert_element_type | solution.py:28
  128.9 4.1 %all-to-all-start.3 = ((bf16[4,512,128]{1,2,0:T(8,128)(2,1)}), bf16[4,512,128]{1,2,0:T(8,128)(2,1)}, u32[]{:S(2)}, u32[]{:S(2)}) async-start(bf16[4,512,128]{1,2,0:T(8,128)(2,1)} %copy.48), calls=%async_computation.3 | async-start | bytes 1048576 | tf_op jit(solution)/shard_map/all_to_all | solution.py:230
  133.1 1.3 copy.56
  134.5 2.0 %fusion.33 = f32[2048,1,128]{0,2,1:T(8,128)S(1)} fusion(f32[2048,1,128]{0,2,1:T(8,128)S(1)} %scatter-add.25, bf16[1,2048,1,128]{3,1,2,0:T(8,128)(2,1)} %copy-done.19, bf16[1,512,1024]{2,1,0:T(8,128)(2,1)} %copy-done.12, f32[512]{0:T(512)} %copy-done.41, f32[1024]{0:T(1024)} %bitcast.267, f32[512]{0:T(512)} %get-tuple-element.151), kind=kOutput, calls=%fused_computation.60 | convolution fusion | flops 137494528 | bytes 2236416 | tf_op jit(solution)/shard_map/htu,thd->uhd/dot_general | solution.py:211
  140.5 4.7 %all-to-all-done.3 = bf16[4,512,128]{1,2,0:T(8,128)(2,1)} async-done(((bf16[4,512,128]{1,2,0:T(8,128)(2,1)}), bf16[4,512,128]{1,2,0:T(8,128)(2,1)}, u32[]{:S(2)}, u32[]{:S(2)}) %all-to-all-start.3) | async-done | bytes 524320 | tf_op jit(solution)/shard_map/all_to_all | solution.py:230
  145.2 3.5 %all-to-all-start.4 = ((bf16[4,512,128]{1,2,0:T(8,128)(2,1)}), bf16[4,512,128]{1,2,0:T(8,128)(2,1)S(1)}, u32[]{:S(2)}, u32[]{:S(2)}) async-start(bf16[4,512,128]{1,2,0:T(8,128)(2,1)} %copy.50), calls=%async_computation.4 | async-start | bytes 1048576 | tf_op jit(solution)/shard_map/all_to_all | solution.py:231
  149.8 11.1 %all-to-all-done.4 = bf16[4,512,128]{1,2,0:T(8,128)(2,1)S(1)} async-done(((bf16[4,512,128]{1,2,0:T(8,128)(2,1)}), bf16[4,512,128]{1,2,0:T(8,128)(2,1)S(1)}, u32[]{:S(2)}, u32[]{:S(2)}) %all-to-all-start.4) | async-done | bytes 524320 | tf_op jit(solution)/shard_map/all_to_all | solution.py:231
  160.9 3.5 %all-to-all-start.5 = ((bf16[4,512,128]{2,1,0:T(8,128)(2,1)}), bf16[4,512,128]{2,1,0:T(8,128)(2,1)S(1)}, u32[]{:S(2)}, u32[]{:S(2)}) async-start(bf16[4,512,128]{2,1,0:T(8,128)(2,1)} %multiply_convert_fusion), calls=%async_computation.5 | async-start | bytes 1048576 | tf_op jit(solution)/shard_map/all_to_all | solution.py:232
  164.4 5.0 %all-gather.2 = bf16[4,1,128]{2,1,0:T(2,128)(2,1)S(1)} all-gather(bf16[1,1,128]{2,1,0:T(2,128)(2,1)S(1)} %bitcast.273), channel_id=2, replica_groups=mesh['grp'=2,'seq'=4,'blk'=2,'rep'=2] {'blk','rep'}, dimensions={0}, use_global_device_ids=true | all-gather | bytes 1280 | tf_op jit(solution)/shard_map/all_gather | solution.py:175
  169.4 5.2 %all-gather.3 = bf16[4,1,2560]{2,1,0:T(2,128)(2,1)S(1)} all-gather(bf16[1,1,2560]{2,1,0:T(2,128)(2,1)S(1)} %bitcast.262), channel_id=1, replica_groups=mesh['grp'=2,'seq'=4,'blk'=2,'rep'=2] {'blk','rep'}, dimensions={0}, use_global_device_ids=true | all-gather | bytes 25600 | tf_op jit(solution)/shard_map/all_gather | solution.py:176
  175.7 1.2 convolution_convert_fusion
  176.9 2.0 %copy.52 = bf16[1,512,512]{2,1,0:T(8,128)(2,1)} copy(bf16[1,512,512]{1,2,0:T(8,128)(2,1)} %bitcast.63) | data formatting | bytes 1048576
  (197 shorter events, 38.4 us)
Async XLA Ops:
  0.6 62.5 %copy-start = (bf16[128,2560]{1,0:T(8,128)(2,1)S(1)}, bf16[128,2560]{1,0:T(8,128)(2,1)}, u32[]{:S(2)}) copy-start(bf16[128,2560]{1,0:T(8,128)(2,1)} %param.34) | copy-start | bytes 1966084
  0.6 26.4 %copy-start.56 = (u32[32]{0:T(128)S(1)}, u32[32]{0:T(128)}, u32[]{:S(2)}) copy-start(u32[32]{0:T(128)} %constant.272) | copy-start | bytes 388
  0.7 8.3 %copy-start.22 = (bf16[1,512,512]{2,1,0:T(8,128)(2,1)S(1)}, bf16[1,512,512]{2,1,0:T(8,128)(2,1)}, u32[]{:S(2)}) copy-start(bf16[1,512,512]{2,1,0:T(8,128)(2,1)} %param.29) | copy-start | bytes 1572868
  0.7 28.9 %copy-start.21 = (bf16[128,2560]{1,0:T(8,128)(2,1)S(1)}, bf16[128,2560]{1,0:T(8,128)(2,1)}, u32[]{:S(2)}) copy-start(bf16[128,2560]{1,0:T(8,128)(2,1)} %param.36) | copy-start | bytes 1966084
  2.7 20.8 %all-to-all-start.1 = ((bf16[512,4,128]{0,2,1:T(8,128)(2,1)}), bf16[512,4,128]{0,2,1:T(8,128)(2,1)S(1)}, u32[]{:S(2)}, u32[]{:S(2)}) async-start(bf16[512,4,128]{0,2,1:T(8,128)(2,1)} %broadcast_in_dim.25), calls=%async_computation.1 | async-start | bytes 1048576 | tf_op jit(solution)/shard_map/all_to_all | solution.py:54
  23.5 17.4 %all-to-all-start = ((bf16[512,4,128]{0,2,1:T(8,128)(2,1)}), bf16[512,4,128]{0,2,1:T(8,128)(2,1)S(1)}, u32[]{:S(2)}, u32[]{:S(2)}) async-start(bf16[512,4,128]{0,2,1:T(8,128)(2,1)} %bitcast), calls=%async_computation | async-start | bytes 1048576 | tf_op jit(solution)/shard_map/all_to_all | solution.py:53
  26.9 14.0 %copy-start.26 = (bf16[1,512,128]{2,1,0:T(8,128)(2,1)S(1)}, bf16[1,512,128]{2,1,0:T(8,128)(2,1)}, u32[]{:S(2)}) copy-start(bf16[1,512,128]{2,1,0:T(8,128)(2,1)} %param.31) | copy-start | bytes 393220
  30.7 17.1 %copy-start.3 = (f32[512,4,128]{2,0,1:T(8,128)}, f32[512,4,128]{2,0,1:T(8,128)S(1)}, u32[]{:S(2)}) copy-start(f32[512,4,128]{2,0,1:T(8,128)S(1)} %convert_element_type.405) | copy-start | bytes 3145732
  41.8 5.8 %copy-start.31 = (f32[128]{0:T(128)S(1)}, f32[128]{0:T(128)}, u32[]{:S(2)}) copy-start(f32[128]{0:T(128)} %param.32) | copy-start | bytes 1540
  41.8 18.3 %all-to-all-start.2 = ((bf16[512,4,128]{2,0,1:T(8,128)(2,1)}), bf16[512,4,128]{2,0,1:T(8,128)(2,1)}, u32[]{:S(2)}, u32[]{:S(2)}) async-start(bf16[512,4,128]{2,0,1:T(8,128)(2,1)} %broadcast_in_dim.29), calls=%async_computation.2 | async-start | bytes 1048576 | tf_op jit(solution)/shard_map/all_to_all | solution.py:55
  57.8 28.9 %copy-start.55 = (f32[128,4]{0,1:T(4,128)S(1)}, f32[128,4]{0,1:T(4,128)}, u32[]{:S(2)}) copy-start(f32[128,4]{0,1:T(4,128)} %param.37) | copy-start | bytes 6148
  88.6 19.3 %copy-start.46 = (f32[128]{0:T(128)}, f32[128]{0:T(128)S(1)}, u32[]{:S(2)}) copy-start(f32[128]{0:T(128)S(1)} %get-tuple-element.139) | copy-start | bytes 1540
  88.6 19.3 %copy-start.48 = (f32[128]{0:T(128)}, f32[128]{0:T(128)S(1)}, u32[]{:S(2)}) copy-start(f32[128]{0:T(128)S(1)} %get-tuple-element.141) | copy-start | bytes 1540
  94.1 9.7 %copy-start.50 = (f32[4]{0:T(128)}, f32[4]{0:T(128)S(1)}, u32[]{:S(2)}) copy-start(f32[4]{0:T(128)S(1)} %get-tuple-element.142) | copy-start | bytes 52
  94.1 9.7 %copy-start.52 = (f32[4]{0:T(128)}, f32[4]{0:T(128)S(1)}, u32[]{:S(2)}) copy-start(f32[4]{0:T(128)S(1)} %get-tuple-element.143) | copy-start | bytes 52
  108.0 7.9 %copy-start.30 = (f32[1,1024]{1,0:T(1,128)}, f32[1,1024]{1,0:T(1,128)S(1)}, u32[]{:S(2)}) copy-start(f32[1,1024]{1,0:T(1,128)S(1)} %slice.261) | copy-start | bytes 12292
  108.6 7.9 %copy-start.16 = (f32[128,512]{1,0:T(8,128)}, f32[128,512]{1,0:T(8,128)S(1)}, u32[]{:S(2)}) copy-start(f32[128,512]{1,0:T(8,128)S(1)} %fusion.60) | copy-start | bytes 786436
  123.9 9.2 %copy-start.6 = (f32[512,4,128]{2,0,1:T(8,128)S(1)}, f32[512,4,128]{2,0,1:T(8,128)}, u32[]{:S(2)}) copy-start(f32[512,4,128]{2,0,1:T(8,128)} %copy-done.3) | copy-start | bytes 3145732
  126.8 7.6 %copy-start.25 = (f32[512,1,128]{0,2,1:T(8,128)S(1)}, f32[512,1,128]{0,2,1:T(8,128)}, u32[]{:S(2)}) copy-start(f32[512,1,128]{0,2,1:T(8,128)} %convolution_bitcast_fusion.3) | copy-start | bytes 786436
  128.9 16.3 %all-to-all-start.3 = ((bf16[4,512,128]{1,2,0:T(8,128)(2,1)}), bf16[4,512,128]{1,2,0:T(8,128)(2,1)}, u32[]{:S(2)}, u32[]{:S(2)}) async-start(bf16[4,512,128]{1,2,0:T(8,128)(2,1)} %copy.48), calls=%async_computation.3 | async-start | bytes 1048576 | tf_op jit(solution)/shard_map/all_to_all | solution.py:230
  139.1 9.6 %copy-start.29 = (f32[2048]{0:T(1024)S(1)}, f32[2048]{0:T(1024)}, u32[]{:S(2)}) copy-start(f32[2048]{0:T(1024)} %get-tuple-element.167) | copy-start | bytes 24580
  139.1 9.6 %copy-start.36 = (f32[128]{0:T(128)S(1)}, f32[128]{0:T(128)}, u32[]{:S(2)}) copy-start(f32[128]{0:T(128)} %copy-done.35) | copy-start | bytes 1540
  139.5 24.9 %copy-start.38 = (bf16[128]{0:T(256)(128)(2,1)S(1)}, bf16[128]{0:T(256)(128)(2,1)}, u32[]{:S(2)}) copy-start(bf16[128]{0:T(256)(128)(2,1)} %copy-done.37) | copy-start | bytes 772
  139.5 29.9 %copy-start.28 = (bf16[1,2560]{1,0:T(2,128)(2,1)S(1)}, bf16[1,2560]{1,0:T(2,128)(2,1)}, u32[]{:S(2)}) copy-start(bf16[1,2560]{1,0:T(2,128)(2,1)} %copy-done.27) | copy-start | bytes 15364
  139.5 35.1 %copy-start.45 = (f32[128]{0:T(128)S(1)}, f32[128]{0:T(128)}, u32[]{:S(2)}) copy-start(f32[128]{0:T(128)} %get-tuple-element.137) | copy-start | bytes 1540
  139.6 35.1 %copy-start.47 = (f32[128]{0:T(128)S(1)}, f32[128]{0:T(128)}, u32[]{:S(2)}) copy-start(f32[128]{0:T(128)} %copy-done.46) | copy-start | bytes 1540
  139.6 35.1 %copy-start.49 = (f32[128]{0:T(128)S(1)}, f32[128]{0:T(128)}, u32[]{:S(2)}) copy-start(f32[128]{0:T(128)} %copy-done.48) | copy-start | bytes 1540
  139.6 35.6 %copy-start.51 = (f32[4]{0:T(128)S(1)}, f32[4]{0:T(128)}, u32[]{:S(2)}) copy-start(f32[4]{0:T(128)} %copy-done.50) | copy-start | bytes 52
  139.6 35.6 %copy-start.53 = (f32[4]{0:T(128)S(1)}, f32[4]{0:T(128)}, u32[]{:S(2)}) copy-start(f32[4]{0:T(128)} %copy-done.52) | copy-start | bytes 52
  139.6 35.6 %copy-start.54 = (f32[4]{0:T(128)S(1)}, f32[4]{0:T(128)}, u32[]{:S(2)}) copy-start(f32[4]{0:T(128)} %get-tuple-element.144) | copy-start | bytes 52
  145.2 15.7 %all-to-all-start.4 = ((bf16[4,512,128]{1,2,0:T(8,128)(2,1)}), bf16[4,512,128]{1,2,0:T(8,128)(2,1)S(1)}, u32[]{:S(2)}, u32[]{:S(2)}) async-start(bf16[4,512,128]{1,2,0:T(8,128)(2,1)} %copy.50), calls=%async_computation.4 | async-start | bytes 1048576 | tf_op jit(solution)/shard_map/all_to_all | solution.py:231
  160.9 18.9 %all-to-all-start.5 = ((bf16[4,512,128]{2,1,0:T(8,128)(2,1)}), bf16[4,512,128]{2,1,0:T(8,128)(2,1)S(1)}, u32[]{:S(2)}, u32[]{:S(2)}) async-start(bf16[4,512,128]{2,1,0:T(8,128)(2,1)} %multiply_convert_fusion), calls=%async_computation.5 | async-start | bytes 1048576 | tf_op jit(solution)/shard_map/all_to_all | solution.py:232
  (31 other events, 56.1 us)
where the time goes:
time: 182 us; the launch traced here: 181 us
  blocking collectives  46 us (25%)
  waiting for transfers between devices  40.6 us (22%)
  starting transfers between devices  25.1 us (14%)
  local copies, waits for them, and re-layouts  23 us (13%)
  other arithmetic  21.8 us (12%)
  matrix products  20.4 us (11%)
  between operations  3.64 us (2%)
    psum x1, blocking collectives, shards(): summed = lax.psum(partial_value, 'seq')  16.8 us
    all_to_all x1, waiting for transfers between devices, shards(): lax.all_to_all(widen(k_proj[0]), 'seq', split_axis=1, concat_axis=0, tile...  12.7 us
    all_to_all x1, waiting for transfers between devices, shards(): lax.all_to_all(k_terms.reshape(flat_shape), 'seq', split_axis=0, concat_a...  11.1 us
    unnamed x120, local copies, waits for them, and re-layouts  10.3 us
    all_to_all x1, waiting for transfers between devices, shards(): lax.all_to_all(q_proj[0], 'seq', split_axis=1, concat_axis=0, tiled=True)  9.79 us
    unnamed x1, blocking collectives  8.26 us
    all_to_all x1, starting transfers between devices, shards(): lax.all_to_all(widen(k_proj[0]), 'seq', split_axis=1, concat_axis=0, tile...  6.32 us
    dot_general x4, matrix products, shards(): jnp.einsum('htu,thd->uhd', grad_logits, q_block[index * block_rows:ending...  5.53 us
  transfers between devices with their start and end apart: 6, of which 5 were waited for; matrix products, arithmetic and copies ran while one was open for 15% of the time, Pallas kernels for 0%

commit v1 on v0

--- a/solution.py
+++ b/solution.py
@@ -3,10 +3,18 @@
 import jax.numpy as jnp
 from jax import lax
 from jax.sharding import PartitionSpec as P
+from jax.lax import all_to_all, axis_size
 
 HD = 128
 PASS_LEN = 2048
 logit_divisor = 0.05
+
+
+def ends_make(payload):
+    part_next = jnp.concatenate(
+        all_to_all(jnp.stack(jnp.split(payload, axis_size("seq"), axis=1)), "seq", 0, 0), axis=0
+    )
+    return part_next
 
 
 def rms_scale(wide):
@@ -52,7 +60,7 @@
     q_heads, k_heads, v_heads = (
         lax.all_to_all(q_proj[0], "seq", split_axis=1, concat_axis=0, tiled=True),
         lax.all_to_all(widen(k_proj[0]), "seq", split_axis=1, concat_axis=0, tiled=True),
-        lax.all_to_all(widen(v_proj[0]), "seq", split_axis=1, concat_axis=0, tiled=True),
+        ends_make(widen(v_proj[0])),
     )
     head_shape = (passes, PASS_LEN, local_heads, HD)
     q_raw = q_heads.reshape(head_shape)

time: 182 us -> 177 us (0.973)
    unnamed x120 -> x123, local copies, waits for them, and re-layouts: 10.3 us -> 9.41 us
    another operation x4 -> x5, other arithmetic: 2.8 us -> 3.66 us
  transfers between devices with their start and end apart: 6 -> 6, of which waited for: 5 -> 5; matrix products, arithmetic and copies ran while one was open for 15% -> 16% of each run, Pallas kernels for 0% -> 0%
where the time goes in v1:
time: 177 us; the launch traced here: 176 us
  blocking collectives  46 us (26%)
  waiting for transfers between devices  39.3 us (22%)
  starting transfers between devices  24.3 us (14%)
  local copies, waits for them, and re-layouts  21.4 us (12%)
  other arithmetic  20.4 us (12%)
  matrix products  20.4 us (12%)
  between operations  3.71 us (2%)
    psum x1, blocking collectives, shards(): summed = lax.psum(partial_value, 'seq')  16.9 us
    all_to_all x1, waiting for transfers between devices, shards(): lax.all_to_all(widen(k_proj[0]), 'seq', split_axis=1, concat_axis=0, tile...  11.5 us
    all_to_all x1, waiting for transfers between devices, shards(): lax.all_to_all(k_terms.reshape(flat_shape), 'seq', split_axis=0, concat_a...  11.1 us
    all_to_all x1, waiting for transfers between devices, shards(): lax.all_to_all(q_proj[0], 'seq', split_axis=1, concat_axis=0, tiled=True)  9.79 us
    unnamed x123, local copies, waits for them, and re-layouts  9.41 us
    unnamed x1, blocking collectives  8.27 us
    all_to_all x1, starting transfers between devices, shards(): lax.all_to_all(widen(k_proj[0]), 'seq', split_axis=1, concat_axis=0, tile...  6.32 us
    dot_general x4, matrix products, shards(): jnp.einsum('htu,thd->uhd', grad_logits, q_block[index * block_rows:ending...  5.54 us
  transfers between devices with their start and end apart: 6, of which 5 were waited for; matrix products, arithmetic and copies ran while one was open for 16% of the time, Pallas kernels for 0%

profile of v1, /device:TPU:0, one launch (start us, length us, event | category | flops | bytes accessed | tf_op | source)
XLA Modules:
  0.0 175.5 jit_solution(7475644404569443490)
XLA Ops:
  2.6 6.3 %all-to-all-start.1 = ((bf16[512,4,128]{0,2,1:T(8,128)(2,1)}), bf16[512,4,128]{0,2,1:T(8,128)(2,1)S(1)}, u32[]{:S(2)}, u32[]{:S(2)}) async-start(bf16[512,4,128]{0,2,1:T(8,128)(2,1)} %broadcast_in_dim.27), calls=%async_computation.1 | async-start | bytes 1048576 | tf_op jit(solution)/shard_map/all_to_all | solution.py:62
  11.9 11.5 %all-to-all-done.1 = bf16[512,4,128]{0,2,1:T(8,128)(2,1)S(1)} async-done(((bf16[512,4,128]{0,2,1:T(8,128)(2,1)}), bf16[512,4,128]{0,2,1:T(8,128)(2,1)S(1)}, u32[]{:S(2)}, u32[]{:S(2)}) %all-to-all-start.1) | async-done | bytes 524320 | tf_op jit(solution)/shard_map/all_to_all | solution.py:62
  23.4 3.5 %all-to-all-start = ((bf16[512,4,128]{0,2,1:T(8,128)(2,1)}), bf16[512,4,128]{0,2,1:T(8,128)(2,1)S(1)}, u32[]{:S(2)}, u32[]{:S(2)}) async-start(bf16[512,4,128]{0,2,1:T(8,128)(2,1)} %bitcast), calls=%async_computation | async-start | bytes 1048576 | tf_op jit(solution)/shard_map/all_to_all | solution.py:61
  31.1 9.8 %all-to-all-done = bf16[512,4,128]{0,2,1:T(8,128)(2,1)S(1)} async-done(((bf16[512,4,128]{0,2,1:T(8,128)(2,1)}), bf16[512,4,128]{0,2,1:T(8,128)(2,1)S(1)}, u32[]{:S(2)}, u32[]{:S(2)}) %all-to-all-start) | async-done | bytes 524320 | tf_op jit(solution)/shard_map/all_to_all | solution.py:61
  40.9 3.5 %all-to-all-start.2 = ((bf16[4,512,128]{2,1,0:T(8,128)(2,1)}), bf16[4,512,128]{2,1,0:T(8,128)(2,1)S(1)}, u32[]{:S(2)}, u32[]{:S(2)}) async-start(bf16[4,512,128]{2,1,0:T(8,128)(2,1)} %pad_maximum_fusion.1), calls=%async_computation.2 | async-start | bytes 1048576 | tf_op jit(solution)/shard_map/all_to_all | solution.py:15
  46.2 1.4 fusion.96
  56.1 2.2 %all-to-all-done.2 = bf16[4,512,128]{2,1,0:T(8,128)(2,1)S(1)} async-done(((bf16[4,512,128]{2,1,0:T(8,128)(2,1)}), bf16[4,512,128]{2,1,0:T(8,128)(2,1)S(1)}, u32[]{:S(2)}, u32[]{:S(2)}) %all-to-all-start.2) | async-done | bytes 524320 | tf_op jit(solution)/shard_map/all_to_all | solution.py:15
  59.4 16.9 %psum.28 = f32[1,2560]{1,0:T(1,128)S(1)} all-reduce(f32[1,2560]{1,0:T(1,128)S(1)} %fusion.77), channel_id=1, replica_groups=mesh['grp'=2,'seq'=4,'blk'=2,'rep'=2] {'seq'}, use_global_device_ids=true, to_apply=%region_11.12 | all-reduce | flops 2560 | bytes 20480 | tf_op jit(solution)/shard_map/psum | solution.py:118
  77.6 5.2 %all-gather.1 = bf16[4,1,2560]{2,1,0:T(2,128)(2,1)S(1)} all-gather(bf16[1,1,2560]{2,1,0:T(2,128)(2,1)S(1)} %convert_bitcast_fusion.1), channel_id=1, replica_groups=mesh['grp'=2,'seq'=4,'blk'=2,'rep'=2] {'blk','rep'}, dimensions={0}, use_global_device_ids=true | all-gather | bytes 25600 | tf_op jit(solution)/shard_map/all_gather | solution.py:121
  82.8 2.0 %fusion.80 = (f32[4]{0:T(128)S(1)}, f32[128]{0:T(128)}, f32[4]{0:T(128)S(1)}, f32[128]{0:T(128)S(1)}, f32[4]{0:T(128)S(1)}, /*index=5*/f32[128]{0:T(128)S(1)}, f32[128,4]{0,1:T(4,128)S(1)}) fusion(f32[128,4]{0,1:T(4,128)S(1)} %copy-done.56, bf16[4,1,2560]{2,1,0:T(2,128)(2,1)S(1)} %all-gather.1, bf16[128,2560]{1,0:T(8,128)(2,1)} %param.36, ...), kind=kOutput, calls=%fused_computation.171 | convolution fusion | flops 3608692 | bytes 682032 | tf_op jit(solution)/shard_map/dot_general | solution.py:129
  84.8 5.4 %all-reduce.3 = (f32[4]{0:T(128)S(1)}, f32[4]{0:T(128)S(1)}, f32[4]{0:T(128)}) all-reduce(f32[4]{0:T(128)S(1)} %get-tuple-element.140, f32[4]{0:T(128)S(1)} %get-tuple-element.138, f32[4]{0:T(128)S(1)} %get-tuple-element.136), channel_id=1, replica_groups=mesh['grp'=2,'seq'=4,'blk'=2,'rep'=2] {'blk'}, use_global_device_ids=true, to_apply=%region_18.19 | all-reduce | flops 12 | bytes 96 | tf_op jit(solution)/shard_map/psum | solution.py:142
  90.2 1.4 fusion.4
  91.6 8.3 %all-reduce.2 = bf16[4,2560]{1,0:T(4,128)(2,1)S(1)} all-reduce(bf16[4,2560]{1,0:T(4,128)(2,1)S(1)} %fusion.4), channel_id=3, replica_groups=mesh['grp'=2,'seq'=4,'blk'=2,'rep'=2] {'blk'}, use_global_device_ids=true, to_apply=%region_19.20.clone | all-reduce | flops 10240 | bytes 40960
  103.6 2.1 %convolution_bitcast_fusion.3 = f32[512,1,128]{0,2,1:T(8,128)} fusion(bf16[1,2048,1,128]{3,1,2,0:T(8,128)(2,1)} %copy-done.20, bf16[1,512,512]{1,2,0:T(8,128)(2,1)S(1)} %copy-done.16, f32[512]{0:T(512)S(1)} %fusion.39, f32[512]{0:T(512)S(1)} %bitcast.275, f32[512]{0:T(512)S(1)} %get-tuple-element.152), kind=kOutput, calls=%fused_computation.63 | convolution fusion | flops 68681728 | bytes 923648 | tf_op jit(solution)/shard_map/htu,thd->uhd/dot_general | solution.py:219
  107.0 1.3 fusion.87
  113.4 2.5 %copy.54 = f32[2048,128]{1,0:T(8,128)} copy(f32[2048,128]{0,1:T(8,128)} %pad_maximum_fusion) | data formatting | bytes 2097152 | tf_op jit(solution)/shard_map/concatenate | solution.py:226
  115.9 1.3 copy.55
  117.2 1.6 fusion.44
  118.9 2.9 %fusion.49 = bf16[4,512,128]{2,1,0:T(8,128)(2,1)} fusion(f32[4,512,128]{2,1,0:T(8,128)} %bitcast.244, bf16[512,4,128]{2,0,1:T(8,128)(2,1)} %copy-done.14, f32[4,512]{1,0:T(4,128)S(1)} %div.160, f32[4,512]{1,0:T(4,128)} %get-tuple-element.151, f32[128]{0:T(128)} %param.32, f32[4,512]{1,0:T(4,128)} %get-tuple-element.149), kind=kLoop, calls=%fused_computation.86 | loop fusion | flops 1835008 | bytes 2122240 | tf_op jit(solution)/shard_map/convert_element_type | solution.py:36
  121.8 2.1 %copy.48 = bf16[4,512,128]{1,2,0:T(8,128)(2,1)} copy(bf16[4,512,128]{2,1,0:T(8,128)(2,1)} %fusion.49) | data formatting | bytes 1048576 | tf_op jit(solution)/shard_map/convert_element_type | solution.py:36
  123.9 4.1 %all-to-all-start.3 = ((bf16[4,512,128]{1,2,0:T(8,128)(2,1)}), bf16[4,512,128]{1,2,0:T(8,128)(2,1)}, u32[]{:S(2)}, u32[]{:S(2)}) async-start(bf16[4,512,128]{1,2,0:T(8,128)(2,1)} %copy.48), calls=%async_computation.3 | async-start | bytes 1048576 | tf_op jit(solution)/shard_map/all_to_all | solution.py:238
  128.0 1.3 copy.56
  129.5 2.0 %fusion.33 = f32[2048,1,128]{0,2,1:T(8,128)S(1)} fusion(f32[2048,1,128]{0,2,1:T(8,128)S(1)} %scatter-add.25, bf16[1,2048,1,128]{3,1,2,0:T(8,128)(2,1)} %copy-done.20, bf16[1,512,1024]{2,1,0:T(8,128)(2,1)} %copy-done.11, f32[512]{0:T(512)} %copy-done.42, f32[1024]{0:T(1024)} %bitcast.272, f32[512]{0:T(512)} %get-tuple-element.155), kind=kOutput, calls=%fused_computation.62 | convolution fusion | flops 137494528 | bytes 2236416 | tf_op jit(solution)/shard_map/htu,thd->uhd/dot_general | solution.py:219
  135.5 4.7 %all-to-all-done.3 = bf16[4,512,128]{1,2,0:T(8,128)(2,1)} async-done(((bf16[4,512,128]{1,2,0:T(8,128)(2,1)}), bf16[4,512,128]{1,2,0:T(8,128)(2,1)}, u32[]{:S(2)}, u32[]{:S(2)}) %all-to-all-start.3) | async-done | bytes 524320 | tf_op jit(solution)/shard_map/all_to_all | solution.py:238
  140.2 3.5 %all-to-all-start.4 = ((bf16[4,512,128]{1,2,0:T(8,128)(2,1)}), bf16[4,512,128]{1,2,0:T(8,128)(2,1)S(1)}, u32[]{:S(2)}, u32[]{:S(2)}) async-start(bf16[4,512,128]{1,2,0:T(8,128)(2,1)} %copy.50), calls=%async_computation.4 | async-start | bytes 1048576 | tf_op jit(solution)/shard_map/all_to_all | solution.py:239
  143.7 1.1 multiply_convert_fusion
  144.8 11.1 %all-to-all-done.4 = bf16[4,512,128]{1,2,0:T(8,128)(2,1)S(1)} async-done(((bf16[4,512,128]{1,2,0:T(8,128)(2,1)}), bf16[4,512,128]{1,2,0:T(8,128)(2,1)S(1)}, u32[]{:S(2)}, u32[]{:S(2)}) %all-to-all-start.4) | async-done | bytes 524320 | tf_op jit(solution)/shard_map/all_to_all | solution.py:239
  155.9 3.5 %all-to-all-start.5 = ((bf16[4,512,128]{2,1,0:T(8,128)(2,1)}), bf16[4,512,128]{2,1,0:T(8,128)(2,1)S(1)}, u32[]{:S(2)}, u32[]{:S(2)}) async-start(bf16[4,512,128]{2,1,0:T(8,128)(2,1)} %multiply_convert_fusion), calls=%async_computation.5 | async-start | bytes 1048576 | tf_op jit(solution)/shard_map/all_to_all | solution.py:240
  159.4 5.0 %all-gather.2 = bf16[4,1,128]{2,1,0:T(2,128)(2,1)S(1)} all-gather(bf16[1,1,128]{2,1,0:T(2,128)(2,1)S(1)} %bitcast.278), channel_id=2, replica_groups=mesh['grp'=2,'seq'=4,'blk'=2,'rep'=2] {'blk','rep'}, dimensions={0}, use_global_device_ids=true | all-gather | bytes 1280 | tf_op jit(solution)/shard_map/all_gather | solution.py:183
  164.4 5.2 %all-gather.3 = bf16[4,1,2560]{2,1,0:T(2,128)(2,1)S(1)} all-gather(bf16[1,1,2560]{2,1,0:T(2,128)(2,1)S(1)} %bitcast.267), channel_id=1, replica_groups=mesh['grp'=2,'seq'=4,'blk'=2,'rep'=2] {'blk','rep'}, dimensions={0}, use_global_device_ids=true | all-gather | bytes 25600 | tf_op jit(solution)/shard_map/all_gather | solution.py:184
  170.7 1.2 convolution_convert_fusion
  171.9 2.0 %copy.52 = bf16[1,512,512]{2,1,0:T(8,128)(2,1)} copy(bf16[1,512,512]{1,2,0:T(8,128)(2,1)} %bitcast.66) | data formatting | bytes 1048576
  (201 shorter events, 35.8 us)
Async XLA Ops:
  0.6 58.6 %copy-start = (bf16[128,2560]{1,0:T(8,128)(2,1)S(1)}, bf16[128,2560]{1,0:T(8,128)(2,1)}, u32[]{:S(2)}) copy-start(bf16[128,2560]{1,0:T(8,128)(2,1)} %param.34) | copy-start | bytes 1966084
  0.6 8.3 %copy-start.23 = (bf16[1,512,512]{2,1,0:T(8,128)(2,1)S(1)}, bf16[1,512,512]{2,1,0:T(8,128)(2,1)}, u32[]{:S(2)}) copy-start(bf16[1,512,512]{2,1,0:T(8,128)(2,1)} %param.29) | copy-start | bytes 1572868
  0.7 9.3 %copy-start.27 = (bf16[1,512,128]{2,1,0:T(8,128)(2,1)S(1)}, bf16[1,512,128]{2,1,0:T(8,128)(2,1)}, u32[]{:S(2)}) copy-start(bf16[1,512,128]{2,1,0:T(8,128)(2,1)} %param.31) | copy-start | bytes 393220
  2.6 20.8 %all-to-all-start.1 = ((bf16[512,4,128]{0,2,1:T(8,128)(2,1)}), bf16[512,4,128]{0,2,1:T(8,128)(2,1)S(1)}, u32[]{:S(2)}, u32[]{:S(2)}) async-start(bf16[512,4,128]{0,2,1:T(8,128)(2,1)} %broadcast_in_dim.27), calls=%async_computation.1 | async-start | bytes 1048576 | tf_op jit(solution)/shard_map/all_to_all | solution.py:62
  10.1 16.9 %copy-start.57 = (u32[32]{0:T(128)S(1)}, u32[32]{0:T(128)}, u32[]{:S(2)}) copy-start(u32[32]{0:T(128)} %constant.272) | copy-start | bytes 388
  10.1 19.4 %copy-start.22 = (bf16[128,2560]{1,0:T(8,128)(2,1)S(1)}, bf16[128,2560]{1,0:T(8,128)(2,1)}, u32[]{:S(2)}) copy-start(bf16[128,2560]{1,0:T(8,128)(2,1)} %param.36) | copy-start | bytes 1966084
  23.4 17.4 %all-to-all-start = ((bf16[512,4,128]{0,2,1:T(8,128)(2,1)}), bf16[512,4,128]{0,2,1:T(8,128)(2,1)S(1)}, u32[]{:S(2)}, u32[]{:S(2)}) async-start(bf16[512,4,128]{0,2,1:T(8,128)(2,1)} %bitcast), calls=%async_computation | async-start | bytes 1048576 | tf_op jit(solution)/shard_map/all_to_all | solution.py:61
  30.7 15.5 %copy-start.3 = (f32[512,4,128]{2,0,1:T(8,128)}, f32[512,4,128]{2,0,1:T(8,128)S(1)}, u32[]{:S(2)}) copy-start(f32[512,4,128]{2,0,1:T(8,128)S(1)} %convert_element_type.401) | copy-start | bytes 3145732
  31.1 14.8 %copy-start.32 = (f32[128]{0:T(128)S(1)}, f32[128]{0:T(128)}, u32[]{:S(2)}) copy-start(f32[128]{0:T(128)} %param.32) | copy-start | bytes 1540
  40.9 17.4 %all-to-all-start.2 = ((bf16[4,512,128]{2,1,0:T(8,128)(2,1)}), bf16[4,512,128]{2,1,0:T(8,128)(2,1)S(1)}, u32[]{:S(2)}, u32[]{:S(2)}) async-start(bf16[4,512,128]{2,1,0:T(8,128)(2,1)} %pad_maximum_fusion.1), calls=%async_computation.2 | async-start | bytes 1048576 | tf_op jit(solution)/shard_map/all_to_all | solution.py:15
  55.0 27.8 %copy-start.56 = (f32[128,4]{0,1:T(4,128)S(1)}, f32[128,4]{0,1:T(4,128)}, u32[]{:S(2)}) copy-start(f32[128,4]{0,1:T(4,128)} %param.37) | copy-start | bytes 6148
  84.8 18.1 %copy-start.47 = (f32[128]{0:T(128)}, f32[128]{0:T(128)S(1)}, u32[]{:S(2)}) copy-start(f32[128]{0:T(128)S(1)} %get-tuple-element.139) | copy-start | bytes 1540
  84.8 18.1 %copy-start.49 = (f32[128]{0:T(128)}, f32[128]{0:T(128)S(1)}, u32[]{:S(2)}) copy-start(f32[128]{0:T(128)S(1)} %get-tuple-element.141) | copy-start | bytes 1540
  90.2 9.7 %copy-start.51 = (f32[4]{0:T(128)}, f32[4]{0:T(128)S(1)}, u32[]{:S(2)}) copy-start(f32[4]{0:T(128)S(1)} %get-tuple-element.142) | copy-start | bytes 52
  90.2 9.7 %copy-start.53 = (f32[4]{0:T(128)}, f32[4]{0:T(128)S(1)}, u32[]{:S(2)}) copy-start(f32[4]{0:T(128)S(1)} %get-tuple-element.143) | copy-start | bytes 52
  102.9 7.9 %copy-start.31 = (f32[1,1024]{1,0:T(1,128)}, f32[1,1024]{1,0:T(1,128)S(1)}, u32[]{:S(2)}) copy-start(f32[1,1024]{1,0:T(1,128)S(1)} %slice.261) | copy-start | bytes 12292
  103.6 7.9 %copy-start.17 = (f32[128,512]{1,0:T(8,128)}, f32[128,512]{1,0:T(8,128)S(1)}, u32[]{:S(2)}) copy-start(f32[128,512]{1,0:T(8,128)S(1)} %fusion.60) | copy-start | bytes 786436
  118.9 9.2 %copy-start.6 = (f32[512,4,128]{2,0,1:T(8,128)S(1)}, f32[512,4,128]{2,0,1:T(8,128)}, u32[]{:S(2)}) copy-start(f32[512,4,128]{2,0,1:T(8,128)} %copy-done.3) | copy-start | bytes 3145732
  121.8 7.6 %copy-start.26 = (f32[512,1,128]{0,2,1:T(8,128)S(1)}, f32[512,1,128]{0,2,1:T(8,128)}, u32[]{:S(2)}) copy-start(f32[512,1,128]{0,2,1:T(8,128)} %convolution_bitcast_fusion.3) | copy-start | bytes 786436
  123.9 16.3 %all-to-all-start.3 = ((bf16[4,512,128]{1,2,0:T(8,128)(2,1)}), bf16[4,512,128]{1,2,0:T(8,128)(2,1)}, u32[]{:S(2)}, u32[]{:S(2)}) async-start(bf16[4,512,128]{1,2,0:T(8,128)(2,1)} %copy.48), calls=%async_computation.3 | async-start | bytes 1048576 | tf_op jit(solution)/shard_map/all_to_all | solution.py:238
  134.1 9.6 %copy-start.30 = (f32[2048]{0:T(1024)S(1)}, f32[2048]{0:T(1024)}, u32[]{:S(2)}) copy-start(f32[2048]{0:T(1024)} %get-tuple-element.171) | copy-start | bytes 24580
  134.1 9.6 %copy-start.37 = (f32[128]{0:T(128)S(1)}, f32[128]{0:T(128)}, u32[]{:S(2)}) copy-start(f32[128]{0:T(128)} %copy-done.36) | copy-start | bytes 1540
  134.5 24.9 %copy-start.39 = (bf16[128]{0:T(256)(128)(2,1)S(1)}, bf16[128]{0:T(256)(128)(2,1)}, u32[]{:S(2)}) copy-start(bf16[128]{0:T(256)(128)(2,1)} %copy-done.38) | copy-start | bytes 772
  134.5 29.9 %copy-start.29 = (bf16[1,2560]{1,0:T(2,128)(2,1)S(1)}, bf16[1,2560]{1,0:T(2,128)(2,1)}, u32[]{:S(2)}) copy-start(bf16[1,2560]{1,0:T(2,128)(2,1)} %copy-done.28) | copy-start | bytes 15364
  134.5 35.1 %copy-start.46 = (f32[128]{0:T(128)S(1)}, f32[128]{0:T(128)}, u32[]{:S(2)}) copy-start(f32[128]{0:T(128)} %get-tuple-element.137) | copy-start | bytes 1540
  134.5 35.1 %copy-start.48 = (f32[128]{0:T(128)S(1)}, f32[128]{0:T(128)}, u32[]{:S(2)}) copy-start(f32[128]{0:T(128)} %copy-done.47) | copy-start | bytes 1540
  134.5 35.1 %copy-start.50 = (f32[128]{0:T(128)S(1)}, f32[128]{0:T(128)}, u32[]{:S(2)}) copy-start(f32[128]{0:T(128)} %copy-done.49) | copy-start | bytes 1540
  134.5 35.6 %copy-start.52 = (f32[4]{0:T(128)S(1)}, f32[4]{0:T(128)}, u32[]{:S(2)}) copy-start(f32[4]{0:T(128)} %copy-done.51) | copy-start | bytes 52
  134.6 35.6 %copy-start.54 = (f32[4]{0:T(128)S(1)}, f32[4]{0:T(128)}, u32[]{:S(2)}) copy-start(f32[4]{0:T(128)} %copy-done.53) | copy-start | bytes 52
  134.6 35.6 %copy-start.55 = (f32[4]{0:T(128)S(1)}, f32[4]{0:T(128)}, u32[]{:S(2)}) copy-start(f32[4]{0:T(128)} %get-tuple-element.144) | copy-start | bytes 52
  140.2 15.7 %all-to-all-start.4 = ((bf16[4,512,128]{1,2,0:T(8,128)(2,1)}), bf16[4,512,128]{1,2,0:T(8,128)(2,1)S(1)}, u32[]{:S(2)}, u32[]{:S(2)}) async-start(bf16[4,512,128]{1,2,0:T(8,128)(2,1)} %copy.50), calls=%async_computation.4 | async-start | bytes 1048576 | tf_op jit(solution)/shard_map/all_to_all | solution.py:239
  155.9 18.9 %all-to-all-start.5 = ((bf16[4,512,128]{2,1,0:T(8,128)(2,1)}), bf16[4,512,128]{2,1,0:T(8,128)(2,1)S(1)}, u32[]{:S(2)}, u32[]{:S(2)}) async-start(bf16[4,512,128]{2,1,0:T(8,128)(2,1)} %multiply_convert_fusion), calls=%async_computation.5 | async-start | bytes 1048576 | tf_op jit(solution)/shard_map/all_to_all | solution.py:240
  (32 other events, 60.0 us)
